TPU v7x, 32 devices: a whole 2x2x4 slice. The times are simulated.
32 devices in a mesh: dom: 8 (over z, x), tensor: 4 (over y, core).
Axes of the slice: x: 2, y: 2, z: 4, core: 2. Of those that a mesh axis runs over, the one named last changes fastest.
Arguments:
- node_state: bfloat16 [2048, 512], P('dom', 'tensor'), may hold values from -6 to 6
- cotangent: bfloat16 [2048, 512], P('dom', 'tensor'), may hold values from -6 to 6
- w_in: bfloat16 [512, 1024], P('tensor'), may hold values from -0.1875 to 0.1875
- w_out: bfloat16 [512, 512], P('tensor'), may hold values from -0.25 to 0.25
- send_list: int32 [8, 7, 16], P('dom'), may hold values from 0 to 255
- sender: int32 [12288], P('dom'), may hold values from 0 to 367
- receiver: int32 [12288], P('dom'), may hold values from 0 to 255
- edge_count: int32 [8], P('dom'), may hold values from 1 to 1536, 6144 in all
Outputs:
- node_grad: bfloat16 [2048, 512], P('dom', 'tensor')
- w_in_grad: float32 [512, 1024], P('tensor')
- w_out_grad: float32 [512, 512], P('tensor')
Inputs may be any that keep to these rules, and one draw needn't show every extreme that they name: `edge_count`: live slots of a partition come first; some partition has all 1536 live.
All inputs are finite; a program needn't handle non-finite values. No bound on the sum of `edge_count` on one device may be relied on, other than what follows from the above.
Results may differ from a plain program's by a relative error of at most 0.0049.
Values may be sent and summed in bfloat16 or wider, within the bound.
A program may use at most 64 MiB of HBM per device.

v0:
```python
import jax
import jax.numpy as jnp
from jax import lax
from jax.sharding import PartitionSpec as P


def shifted(value, axis, steps):
    count = lax.axis_size(axis)
    pairs = [(source, (source + steps) % count) for source in range(count)]
    return lax.ppermute(value, axis, pairs)


def contract_rows(left, right):
    return lax.dot_general(
        left, right, (((0,), (0,)), ((), ())), preferred_element_type=jnp.float32
    )


def contract_cols(left, right):
    return lax.dot_general(
        left, right, (((1,), (1,)), ((), ())), preferred_element_type=jnp.float32
    )


def neighbour_offsets(count):
    return [1, count - 1, 2, count - 2, 3, count - 3, count // 2]


def per_device(node_state, cotangent, w_in, w_out, send_list, sender, receiver, edge_count):
    local_rows = node_state.shape[0]
    slots = send_list.shape[2]
    peers = send_list.shape[1]
    parts = lax.axis_size("dom")
    offsets = neighbour_offsets(parts)
    my_list = send_list[0]
    arrived = []
    for which, offset in enumerate(offsets):
        arrived.append(shifted(node_state[my_list[which]], "dom", offset))
    incoming = jnp.concatenate(arrived, 0)
    table_part = jnp.concatenate([node_state, incoming], 0)
    table, cot_full = (
        lax.all_gather(table_part, "tensor", axis=1, tiled=True),
        lax.all_gather(cotangent, "tensor", axis=1, tiled=True),
    )
    width = table.shape[1]
    rows = table.shape[0]
    w_send = w_in[:, :width]
    w_recv = w_in[:, width:]
    sent = table[sender]
    recv = table[receiver]
    pre = contract_cols(sent, w_send) + contract_cols(recv, w_recv)
    sig = jax.nn.sigmoid(pre)
    act = (pre * sig).astype(jnp.bfloat16)
    slope = sig * (1.0 + pre * (1.0 - sig))
    live = (jnp.arange(sender.shape[0], dtype=jnp.int32) < edge_count[0]).astype(jnp.bfloat16)
    message_grad = cot_full[receiver] * live[:, None]
    out_grad = contract_rows(act, message_grad)
    hidden_grad = contract_cols(message_grad, w_out)
    pre_grad = (hidden_grad * slope).astype(jnp.bfloat16)
    in_grad = jnp.concatenate([contract_rows(pre_grad, sent), contract_rows(pre_grad, recv)], 1)
    hit_send = (sender[:, None] == jnp.arange(rows, dtype=jnp.int32)[None, :]).astype(jnp.bfloat16)
    hit_recv = (receiver[:, None] == jnp.arange(local_rows, dtype=jnp.int32)[None, :]).astype(
        jnp.bfloat16
    )
    send_sum = contract_rows(hit_send, pre_grad).astype(jnp.bfloat16)
    recv_sum = contract_rows(hit_recv, pre_grad).astype(jnp.bfloat16)
    term = jnp.dot(send_sum, w_send, preferred_element_type=jnp.float32)
    term = term.at[:local_rows].add(jnp.dot(recv_sum, w_recv, preferred_element_type=jnp.float32))
    row_grad = lax.psum_scatter(term, "tensor", scatter_dimension=1, tiled=True)
    feat_part = row_grad.shape[1]
    halo_grad = row_grad[local_rows:].reshape(peers, slots, feat_part)
    node_grad = cotangent.astype(jnp.float32) + row_grad[:local_rows]
    for which, offset in enumerate(offsets):
        returned = shifted(halo_grad[which], "dom", parts - offset)
        node_grad = node_grad.at[my_list[which]].add(returned)
    sum_in, sum_out = lax.psum((in_grad, out_grad), "dom")
    scale = float(sender.shape[0] * parts) ** (-0.5)
    return (node_grad.astype(jnp.bfloat16), sum_in * scale, sum_out * scale)


def solution(mesh):
    return jax.shard_map(
        per_device,
        mesh=mesh,
        in_specs=(
            P("dom", "tensor"),
            P("dom", "tensor"),
            P("tensor", None),
            P("tensor", None),
            P("dom", None, None),
            P("dom"),
            P("dom"),
            P("dom"),
        ),
        out_specs=(P("dom", "tensor"), P("tensor", None), P("tensor", None)),
        check_vma=False,
    )
```

profile of v0, /device:TPU:0, one launch (start us, length us, event | category | flops | bytes accessed | tf_op | source)
XLA Modules:
  0.0 181.0 jit_solution(16748766405310183647)
XLA Ops:
  8.1 0.8 fusion.28
  8.9 1.4 gather_fusion.6
  10.3 5.0 %collective-permute-start.5 = (bf16[16,128]{1,0:T(8,128)(2,1)S(1)}, bf16[16,128]{1,0:T(8,128)(2,1)S(1)}, u32[]{:S(2)}, u32[]{:S(2)}) collective-permute-start(bf16[16,128]{1,0:T(8,128)(2,1)S(1)} %gather_fusion.6), channel_id=1, source_target_pairs={{0,20},{4,24},{8,28},{12,0},{16,4},{20,8},{24,12},{28,16},{1,21},{... | collective-permute-start | bytes 12296 | tf_op jit(solution)/shard_map/ppermute | solution.py:10
  15.3 1.4 gather_fusion.1
  16.7 1.6 collective-permute-start
  18.3 1.4 gather_fusion.2
  19.7 3.2 %collective-permute-start.1 = (bf16[16,128]{1,0:T(8,128)(2,1)S(1)}, bf16[16,128]{1,0:T(8,128)(2,1)S(1)}, u32[]{:S(2)}, u32[]{:S(2)}) collective-permute-start(bf16[16,128]{1,0:T(8,128)(2,1)S(1)} %gather_fusion.2), channel_id=1, source_target_pairs={{0,28},{4,0},{8,4},{12,8},{16,12},{20,16},{24,20},{28,24},{1,29},{... | collective-permute-start | bytes 12296 | tf_op jit(solution)/shard_map/ppermute | solution.py:10
  23.0 1.4 gather_fusion.3
  24.4 1.4 gather_fusion.4
  25.9 3.8 %collective-permute-start.3 = (bf16[16,128]{1,0:T(8,128)(2,1)S(1)}, bf16[16,128]{1,0:T(8,128)(2,1)S(1)}, u32[]{:S(2)}, u32[]{:S(2)}) collective-permute-start(bf16[16,128]{1,0:T(8,128)(2,1)S(1)} %gather_fusion.4), channel_id=1, source_target_pairs={{0,24},{4,28},{8,0},{12,4},{16,8},{20,12},{24,16},{28,20},{1,25},{... | collective-permute-start | bytes 12296 | tf_op jit(solution)/shard_map/ppermute | solution.py:10
  29.7 0.8 constant_dynamic-update-slice_fusion.7
  31.3 0.7 compare_select_fusion.2
  32.0 0.7 compare_select_fusion
  32.7 6.0 %all_gather.6 = bf16[256,512]{1,0:T(8,128)(2,1)S(1)} all-gather(bf16[256,128]{1,0:T(8,128)(2,1)} %param.11), channel_id=1, replica_groups=mesh['dom'=8,'tensor'=4] {'tensor'}, dimensions={1}, use_global_device_ids=true | all-gather | bytes 327680 | tf_op jit(solution)/shard_map/all_gather | solution.py:43
  38.7 1.4 gather_fusion.7
  40.1 1.4 gather_fusion.5
  41.5 5.4 %gather_fusion = bf16[1536,512]{1,0:T(8,128)(2,1)} fusion(bf16[256,512]{1,0:T(8,128)(2,1)S(1)} %all_gather.6, s32[2048]{0:T(1024)S(1)} %pad_clamp_fusion.2), kind=kCustom, calls=%fused_computation | custom fusion | bytes 3151872 | tf_op jit(solution)/shard_map/gather | solution.py:56
  47.1 5.3 %collective-permute-done.4 = bf16[16,128]{1,0:T(8,128)(2,1)S(1)} collective-permute-done((bf16[16,128]{1,0:T(8,128)(2,1)S(1)}, bf16[16,128]{1,0:T(8,128)(2,1)S(1)}, u32[]{:S(2)}, u32[]{:S(2)}) %collective-permute-start.4) | collective-permute-done | bytes 4128 | tf_op jit(solution)/shard_map/ppermute | solution.py:10
  52.4 6.4 %all_gather.7 = bf16[368,512]{1,0:T(8,128)(2,1)S(1)} all-gather(bf16[368,128]{1,0:T(8,128)(2,1)S(1)} %constant_dynamic-update-slice_fusion), channel_id=1, replica_groups=mesh['dom'=8,'tensor'=4] {'tensor'}, dimensions={1}, use_global_device_ids=true | all-gather | bytes 471040 | tf_op jit(solution)/shard_map/all_gather | solution.py:42
  58.8 4.8 %gather_fusion.9 = bf16[1536,512]{1,0:T(8,128)(2,1)S(1)} fusion(bf16[368,512]{1,0:T(8,128)(2,1)S(1)} %all_gather.7, s32[2048]{0:T(1024)S(1)} %get-tuple-element.33), kind=kCustom, calls=%fused_computation.9 | custom fusion | bytes 3151872 | tf_op jit(solution)/shard_map/gather | solution.py:50
  63.6 5.4 %gather_fusion.8 = bf16[1536,512]{1,0:T(8,128)(2,1)} fusion(bf16[368,512]{1,0:T(8,128)(2,1)S(1)} %all_gather.7, s32[2048]{0:T(1024)S(1)} %get-tuple-element.34), kind=kCustom, calls=%fused_computation.8 | custom fusion | bytes 3151872 | tf_op jit(solution)/shard_map/gather | solution.py:49
  69.6 0.8 copy-done.1
  70.5 0.6 convolution_add_fusion
  71.0 0.8 copy-done.3
  71.9 1.4 fusion.3
  73.2 0.6 fusion
  74.7 0.8 pad_maximum_fusion
  75.6 1.2 fusion.10
  76.9 1.0 fusion.6
  77.9 0.9 copy-done.2
  78.8 71.1 %all-reduce.3.cloned.1.call-done = (f32[128,1024]{1,0:T(8,128)}, f32[128,512]{1,0:T(8,128)}) async-done(((f32[128,1024]{1,0:T(8,128)}, f32[128,512]{1,0:T(8,128)}), (f32[128,1024]{1,0:T(8,128)}, f32[128,512]{1,0:T(8,128)})) %all-reduce.3.cloned.1.call-update) | async-done | bytes 786448 | tf_op jit(solution)/shard_map/psum | solution.py:76
  149.9 1.9 %broadcast_multiply_fusion = f32[128,1024]{1,0:T(8,128)} fusion(f32[128,1024]{1,0:T(8,128)} %get-tuple-element.15), kind=kLoop, calls=%fused_computation.40 | loop fusion | flops 131072 | bytes 1048576 | tf_op jit(solution)/shard_map/mul | solution.py:78
  151.8 0.8 fusion.30
  152.6 0.7 collective-permute-start.8
  153.3 4.1 %collective-permute-start.7 = (f32[16,128]{1,0:T(8,128)S(1)}, f32[16,128]{1,0:T(8,128)S(1)}, u32[]{:S(2)}, u32[]{:S(2)}) collective-permute-start(f32[16,128]{1,0:T(8,128)S(1)} %get-tuple-element.23), channel_id=1, source_target_pairs={{0,28},{4,0},{8,4},{12,8},{16,12},{20,16},{24,20},{28,24},{1,29},{... | collective-permute-start | bytes 24584 | tf_op jit(solution)/shard_map/ppermute | solution.py:10
  157.4 1.7 broadcast_multiply_fusion.1
  159.6 3.3 %collective-permute-start.11 = (f32[16,128]{1,0:T(8,128)S(1)}, f32[16,128]{1,0:T(8,128)S(1)}, u32[]{:S(2)}, u32[]{:S(2)}) collective-permute-start(f32[16,128]{1,0:T(8,128)S(1)} %get-tuple-element.19), channel_id=1, source_target_pairs={{0,20},{4,24},{8,28},{12,0},{16,4},{20,8},{24,12},{28,16},{1,21},{... | collective-permute-start | bytes 24584 | tf_op jit(solution)/shard_map/ppermute | solution.py:10
  162.9 1.0 collective-permute-start.10
  163.8 2.9 %collective-permute-start.9 = (f32[16,128]{1,0:T(8,128)S(1)}, f32[16,128]{1,0:T(8,128)S(1)}, u32[]{:S(2)}, u32[]{:S(2)}) collective-permute-start(f32[16,128]{1,0:T(8,128)S(1)} %get-tuple-element.21), channel_id=1, source_target_pairs={{0,24},{4,28},{8,0},{12,4},{16,8},{20,12},{24,16},{28,20},{1,25},{... | collective-permute-start | bytes 24584 | tf_op jit(solution)/shard_map/ppermute | solution.py:10
  166.7 0.9 slice_add_fusion
  167.6 0.7 scatter_fusion
  168.4 0.7 scatter_fusion.1
  169.1 0.7 scatter_fusion.2
  169.9 0.7 scatter_fusion.3
  170.6 0.7 scatter_fusion.4
  171.4 0.7 scatter_fusion.5
  172.1 0.7 scatter_fusion.6
  172.9 0.6 convert_element_type.32
  (56 shorter events, 2.4 us)
Async XLA Ops:
  8.0 65.2 %copy-start = (bf16[128,512]{1,0:T(8,128)(2,1)S(1)}, bf16[128,512]{1,0:T(8,128)(2,1)}, u32[]{:S(2)}) copy-start(bf16[128,512]{1,0:T(8,128)(2,1)} %param.13) | copy-start | bytes 393220
  8.0 141.9 %all-reduce.3.cloned.1.call-start = ((), (), s32[]{:S(2)}) async-start(), calls=%async_computation.2 | async-start | bytes 1572864 | tf_op jit(solution)/shard_map/psum | solution.py:76
  10.3 42.1 %collective-permute-start.5 = (bf16[16,128]{1,0:T(8,128)(2,1)S(1)}, bf16[16,128]{1,0:T(8,128)(2,1)S(1)}, u32[]{:S(2)}, u32[]{:S(2)}) collective-permute-start(bf16[16,128]{1,0:T(8,128)(2,1)S(1)} %gather_fusion.6), channel_id=1, source_target_pairs={{0,20},{4,24},{8,28},{12,0},{16,4},{20,8},{24,12},{28,16},{1,21},{... | collective-permute-start | bytes 12296 | tf_op jit(solution)/shard_map/ppermute | solution.py:10
  16.7 30.2 %collective-permute-start = (bf16[16,128]{1,0:T(8,128)(2,1)S(1)}, bf16[16,128]{1,0:T(8,128)(2,1)S(1)}, u32[]{:S(2)}, u32[]{:S(2)}) collective-permute-start(bf16[16,128]{1,0:T(8,128)(2,1)S(1)} %gather_fusion.1), channel_id=1, source_target_pairs={{0,4},{4,8},{8,12},{12,16},{16,20},{20,24},{24,28},{28,0},{1,5},{5... | collective-permute-start | bytes 12296 | tf_op jit(solution)/shard_map/ppermute | solution.py:10
  19.7 27.2 %collective-permute-start.1 = (bf16[16,128]{1,0:T(8,128)(2,1)S(1)}, bf16[16,128]{1,0:T(8,128)(2,1)S(1)}, u32[]{:S(2)}, u32[]{:S(2)}) collective-permute-start(bf16[16,128]{1,0:T(8,128)(2,1)S(1)} %gather_fusion.2), channel_id=1, source_target_pairs={{0,28},{4,0},{8,4},{12,8},{16,12},{20,16},{24,20},{28,24},{1,29},{... | collective-permute-start | bytes 12296 | tf_op jit(solution)/shard_map/ppermute | solution.py:10
  24.4 22.7 %collective-permute-start.2 = (bf16[16,128]{1,0:T(8,128)(2,1)S(1)}, bf16[16,128]{1,0:T(8,128)(2,1)S(1)}, u32[]{:S(2)}, u32[]{:S(2)}) collective-permute-start(bf16[16,128]{1,0:T(8,128)(2,1)S(1)} %gather_fusion.3), channel_id=1, source_target_pairs={{0,8},{4,12},{8,16},{12,20},{16,24},{20,28},{24,0},{28,4},{1,9},{5... | collective-permute-start | bytes 12296 | tf_op jit(solution)/shard_map/ppermute | solution.py:10
  25.9 21.2 %collective-permute-start.3 = (bf16[16,128]{1,0:T(8,128)(2,1)S(1)}, bf16[16,128]{1,0:T(8,128)(2,1)S(1)}, u32[]{:S(2)}, u32[]{:S(2)}) collective-permute-start(bf16[16,128]{1,0:T(8,128)(2,1)S(1)} %gather_fusion.4), channel_id=1, source_target_pairs={{0,24},{4,28},{8,0},{12,4},{16,8},{20,12},{24,16},{28,20},{1,25},{... | collective-permute-start | bytes 12296 | tf_op jit(solution)/shard_map/ppermute | solution.py:10
  46.9 5.4 %collective-permute-start.4 = (bf16[16,128]{1,0:T(8,128)(2,1)S(1)}, bf16[16,128]{1,0:T(8,128)(2,1)S(1)}, u32[]{:S(2)}, u32[]{:S(2)}) collective-permute-start(bf16[16,128]{1,0:T(8,128)(2,1)S(1)} %gather_fusion.5), channel_id=1, source_target_pairs={{0,12},{4,16},{8,20},{12,24},{16,28},{20,0},{24,4},{28,8},{1,13},{... | collective-permute-start | bytes 12296 | tf_op jit(solution)/shard_map/ppermute | solution.py:10
  47.0 5.4 %collective-permute-start.6 = (bf16[16,128]{1,0:T(8,128)(2,1)S(1)}, bf16[16,128]{1,0:T(8,128)(2,1)S(1)}, u32[]{:S(2)}, u32[]{:S(2)}) collective-permute-start(bf16[16,128]{1,0:T(8,128)(2,1)S(1)} %gather_fusion.7), channel_id=1, source_target_pairs={{0,16},{4,20},{8,24},{12,28},{16,0},{20,4},{24,8},{28,12},{1,17},{... | collective-permute-start | bytes 12296 | tf_op jit(solution)/shard_map/ppermute | solution.py:10
  63.6 5.4 %copy-start.4 = (bf16[128,1024]{1,0:T(8,128)(2,1)S(1)}, bf16[128,1024]{1,0:T(8,128)(2,1)}, u32[]{:S(2)}) copy-start(bf16[128,1024]{1,0:T(8,128)(2,1)} %param.12) | copy-start | bytes 786436
  69.1 1.4 copy-start.1
  70.5 1.4 copy-start.3
  74.3 1.3 copy-start.7
  74.7 2.2 %copy-start.6 = (s32[1536]{0:T(1024)S(1)}, s32[1536]{0:T(1024)}, u32[]{:S(2)}) copy-start(s32[1536]{0:T(1024)} %param.16) | copy-start | bytes 18436
  75.6 76.3 %reduce-scatter.2.cloned.1.call-start = ((), (), s32[]{:S(2)}) async-start(), calls=%async_computation.1 | async-start | bytes 942080 | tf_op jit(solution)/shard_map/reduce_scatter | solution.py:69
  77.9 0.9 copy-start.2
  77.9 88.8 %copy-start.5 = (bf16[256,128]{1,0:T(8,128)(2,1)S(1)}, bf16[256,128]{1,0:T(8,128)(2,1)}, u32[]{:S(2)}) copy-start(bf16[256,128]{1,0:T(8,128)(2,1)} %param.11) | copy-start | bytes 196612
  152.6 10.2 %collective-permute-start.8 = (f32[16,128]{1,0:T(8,128)S(1)}, f32[16,128]{1,0:T(8,128)S(1)}, u32[]{:S(2)}, u32[]{:S(2)}) collective-permute-start(f32[16,128]{1,0:T(8,128)S(1)} %get-tuple-element.22), channel_id=1, source_target_pairs={{0,4},{4,8},{8,12},{12,16},{16,20},{20,24},{24,28},{28,0},{1,5},{5... | collective-permute-start | bytes 24584 | tf_op jit(solution)/shard_map/ppermute | solution.py:10
  153.3 10.6 %collective-permute-start.7 = (f32[16,128]{1,0:T(8,128)S(1)}, f32[16,128]{1,0:T(8,128)S(1)}, u32[]{:S(2)}, u32[]{:S(2)}) collective-permute-start(f32[16,128]{1,0:T(8,128)S(1)} %get-tuple-element.23), channel_id=1, source_target_pairs={{0,28},{4,0},{8,4},{12,8},{16,12},{20,16},{24,20},{28,24},{1,29},{... | collective-permute-start | bytes 24584 | tf_op jit(solution)/shard_map/ppermute | solution.py:10
  159.0 13.1 %collective-permute-start.13 = (f32[16,128]{1,0:T(8,128)S(1)}, f32[16,128]{1,0:T(8,128)S(1)}, u32[]{:S(2)}, u32[]{:S(2)}) collective-permute-start(f32[16,128]{1,0:T(8,128)S(1)} %get-tuple-element.17), channel_id=1, source_target_pairs={{0,16},{4,20},{8,24},{12,28},{16,0},{20,4},{24,8},{28,12},{1,17},{... | collective-permute-start | bytes 24584 | tf_op jit(solution)/shard_map/ppermute | solution.py:10
  159.0 12.3 %collective-permute-start.12 = (f32[16,128]{1,0:T(8,128)S(1)}, f32[16,128]{1,0:T(8,128)S(1)}, u32[]{:S(2)}, u32[]{:S(2)}) collective-permute-start(f32[16,128]{1,0:T(8,128)S(1)} %get-tuple-element.18), channel_id=1, source_target_pairs={{0,12},{4,16},{8,20},{12,24},{16,28},{20,0},{24,4},{28,8},{1,13},{... | collective-permute-start | bytes 24584 | tf_op jit(solution)/shard_map/ppermute | solution.py:10
  159.6 11.0 %collective-permute-start.11 = (f32[16,128]{1,0:T(8,128)S(1)}, f32[16,128]{1,0:T(8,128)S(1)}, u32[]{:S(2)}, u32[]{:S(2)}) collective-permute-start(f32[16,128]{1,0:T(8,128)S(1)} %get-tuple-element.19), channel_id=1, source_target_pairs={{0,20},{4,24},{8,28},{12,0},{16,4},{20,8},{24,12},{28,16},{1,21},{... | collective-permute-start | bytes 24584 | tf_op jit(solution)/shard_map/ppermute | solution.py:10
  162.9 7.0 %collective-permute-start.10 = (f32[16,128]{1,0:T(8,128)S(1)}, f32[16,128]{1,0:T(8,128)S(1)}, u32[]{:S(2)}, u32[]{:S(2)}) collective-permute-start(f32[16,128]{1,0:T(8,128)S(1)} %get-tuple-element.20), channel_id=1, source_target_pairs={{0,8},{4,12},{8,16},{12,20},{16,24},{20,28},{24,0},{28,4},{1,9},{5... | collective-permute-start | bytes 24584 | tf_op jit(solution)/shard_map/ppermute | solution.py:10
  163.8 5.3 %collective-permute-start.9 = (f32[16,128]{1,0:T(8,128)S(1)}, f32[16,128]{1,0:T(8,128)S(1)}, u32[]{:S(2)}, u32[]{:S(2)}) collective-permute-start(f32[16,128]{1,0:T(8,128)S(1)} %get-tuple-element.21), channel_id=1, source_target_pairs={{0,24},{4,28},{8,0},{12,4},{16,8},{20,12},{24,16},{28,20},{1,25},{... | collective-permute-start | bytes 24584 | tf_op jit(solution)/shard_map/ppermute | solution.py:10
Sparse Core Ops, SparseCore 0:
  75.7 74.1 all-reduce.2
Sparse Core Ops, SparseCore 1:
  78.9 22.2 reduce-scatter.1
where the time goes:
time: 182 us; the launch traced here: 181 us
  waiting for transfers between devices  76.4 us (42%)
  local copies, waits for them, and re-layouts  29.8 us (16%)
  starting transfers between devices  26.3 us (14%)
  between operations  16.5 us (9%)
  other arithmetic  13.4 us (7%)
  blocking collectives  12.4 us (7%)
  matrix products  6.18 us (3%)
    psum x1, waiting for transfers between devices, per_device(): sum_in, sum_out = lax.psum((in_grad, out_grad), 'dom')  71.1 us
    ppermute x14, starting transfers between devices, shifted(): return lax.ppermute(value, axis, pairs)  26.2 us
    gather x7, local copies, waits for them, and re-layouts, per_device(): arrived.append(shifted(node_state[my_list[which]], 'dom', offset))  9.91 us
    all_gather x1, blocking collectives, per_device(): lax.all_gather(table_part, 'tensor', axis=1, tiled=True)  6.42 us
    all_gather x1, blocking collectives, per_device(): lax.all_gather(cotangent, 'tensor', axis=1, tiled=True)  6.03 us
    gather x1, local copies, waits for them, and re-layouts, per_device(): sent = table[sender]  5.42 us
    gather x1, local copies, waits for them, and re-layouts, per_device(): message_grad = cot_full[receiver] * live[:, None]  5.4 us
    ppermute x14, waiting for transfers between devices, shifted(): return lax.ppermute(value, axis, pairs)  5.29 us
  transfers between devices with their start and end apart: 16, of which 2 were waited for; matrix products, arithmetic and copies ran while one was open for 15% of the time, Pallas kernels for 0%

commit v1 on v0

--- a/solution.py
+++ b/solution.py
@@ -1,6 +1,10 @@
+import functools
+
 import jax
 import jax.numpy as jnp
 from jax import lax
+from jax.experimental import pallas as pl
+from jax.experimental.pallas import tpu as pltpu
 from jax.sharding import PartitionSpec as P
 
 
@@ -78,9 +82,283 @@
     return (node_grad.astype(jnp.bfloat16), sum_in * scale, sum_out * scale)
 
 
+MESH = pl.DeviceIdType.MESH
+
+
+def dot(left, right):
+    return jnp.dot(left, right, preferred_element_type=jnp.float32)
+
+
+def split(value):
+    high = value.astype(jnp.bfloat16)
+    low = (value - high.astype(jnp.float32)).astype(jnp.bfloat16)
+    return jnp.concatenate([high, low], 0)
+
+
+def layer_kernel(
+    parts, tps, offsets, slots, scale,
+    x_ref, c_ref, win_ref, wout_ref, list_ref, send_ref, recv_ref, count_ref,
+    node_ref, gin_ref, gout_ref,
+    xf, cf, st_loc, st_hal, rt, lt, ap, pre_buf, hid_buf,
+    halo_out, halo_in, back_out, back_in, sums, rs, ag_out, ag, part_f, part_b, part_in,
+    gx_s, gx_r, gc_s, gc_r, h_s, h_r, b_s, b_r, rs_s, rs_r, ag_s, ag_r, p_s, p_r,
+):
+    me = lax.axis_index("dom")
+    mt = lax.axis_index("tensor")
+    rows, feat = x_ref.shape
+    hid = win_ref.shape[0]
+    width = feat * tps
+    edges = send_ref.shape[1]
+    peers = len(offsets)
+    halos = peers * slots
+    chunk = hid // parts
+    tile = 512 if edges % 512 == 0 else edges
+    tiles = [slice(i, i + tile) for i in range(0, edges, tile)]
+
+    def mod(value, count):
+        return lax.rem(value + count, count)
+
+    def copy(src, dst, ss, rsem, **where):
+        return pltpu.make_async_remote_copy(
+            src_ref=src, dst_ref=dst, send_sem=ss, recv_sem=rsem,
+            device_id=where, device_id_type=MESH,
+        )
+
+    barrier = pltpu.get_barrier_semaphore()
+    for k in range(1, tps):
+        pl.semaphore_signal(barrier, inc=1, device_id={"tensor": mod(mt + k, tps)}, device_id_type=MESH)
+    for k in range(1, parts):
+        pl.semaphore_signal(barrier, inc=1, device_id={"dom": mod(me + k, parts)}, device_id_type=MESH)
+    pl.semaphore_wait(barrier, tps - 1 + parts - 1)
+
+    mine = pl.ds(pl.multiple_of(mt * feat, feat), feat)
+    x_copies = [
+        copy(x_ref, xf.at[:, mine], gx_s.at[k], gx_r.at[k], tensor=mod(mt + k, tps))
+        for k in range(1, tps)
+    ]
+    c_copies = [
+        copy(c_ref, cf.at[:, mine], gc_s.at[k], gc_r.at[k], tensor=mod(mt + k, tps))
+        for k in range(1, tps)
+    ]
+    for item in x_copies + c_copies:
+        item.start()
+    xf[:, mine] = x_ref[...]
+    cf[:, mine] = c_ref[...]
+
+    def hits(index, first, count):
+        lanes = index.shape[1]
+        spot = lax.broadcasted_iota(jnp.int32, (count, lanes), 0) + first
+        return jnp.where(spot == index, 1.0, 0.0).astype(jnp.bfloat16)
+
+    lt[...] = hits(list_ref[...], 0, rows)
+    count = count_ref[0]
+    for cols in tiles:
+        where = lax.broadcasted_iota(jnp.int32, (1, tile), 1) + cols.start
+        target = jnp.where(where < count, recv_ref[:, cols], -1)
+        rt[:, cols] = hits(target, 0, rows)
+        st_loc[:, cols] = hits(send_ref[:, cols], 0, rows)
+        st_hal[:, cols] = hits(send_ref[:, cols], rows, halos)
+
+    for item in x_copies:
+        item.wait_recv()
+    own = split(contract_cols(win_ref[:, :width], xf[...]))
+    picked = dot(own, lt[...])
+    halo_out[...] = (picked[:hid] + picked[hid:]).T
+    h_copies = []
+    for j, offset in enumerate(offsets):
+        band = slice(j * slots, (j + 1) * slots)
+        item = copy(
+            halo_out.at[band], halo_in.at[band], h_s.at[j], h_r.at[j],
+            dom=mod(me + offset, parts),
+        )
+        item.start()
+        h_copies.append(item)
+
+    at_recv = split(contract_cols(win_ref[:, width:], xf[...]))
+    for cols in tiles:
+        both = dot(own, st_loc[:, cols]) + dot(at_recv, rt[:, cols])
+        pre_buf[:, cols] = both[:hid] + both[hid:]
+    for item in c_copies:
+        item.wait_recv()
+    grad = split(contract_cols(wout_ref[...], cf[...]))
+    for cols in tiles:
+        both = dot(grad, rt[:, cols])
+        hid_buf[:, cols] = both[:hid] + both[hid:]
+
+    for item in h_copies:
+        item.wait_recv()
+    far = split(halo_in[...].T)
+    for cols in tiles:
+        both = dot(far, st_hal[:, cols])
+        pre = pre_buf[:, cols] + both[:hid] + both[hid:]
+        sig = jax.nn.sigmoid(pre)
+        slope = sig * (1.0 + pre * (1.0 - sig))
+        ap[:hid, cols] = (pre * sig).astype(jnp.bfloat16)
+        ap[hid:, cols] = (hid_buf[:, cols] * slope).astype(jnp.bfloat16)
+
+    back_out[...] = contract_cols(st_hal[...], ap[hid:]).astype(jnp.bfloat16)
+    b_copies = []
+    for j, offset in enumerate(offsets):
+        band = slice(j * slots, (j + 1) * slots)
+        item = copy(
+            back_out.at[band], back_in.at[band], b_s.at[j], b_r.at[j],
+            dom=mod(me - offset, parts),
+        )
+        item.start()
+        b_copies.append(item)
+
+    spans = [slice(width, 3 * width), slice(0, width)]
+
+    def scatter(which):
+        out = []
+        for k in range(1, parts):
+            peer = mod(me + k, parts)
+            band = pl.ds(pl.multiple_of(peer * chunk, chunk), chunk)
+            item = copy(
+                sums.at[band, spans[which]], rs.at[k, :, spans[which]],
+                rs_s.at[which, k], rs_r.at[which, k], dom=peer,
+            )
+            item.start()
+            out.append(item)
+        return out
+
+    ours = pl.ds(pl.multiple_of(me * chunk, chunk), chunk)
+
+    def reduce(which, arrivals):
+        span = spans[which]
+        total = sums[ours, span].astype(jnp.float32)
+        for k, item in enumerate(arrivals):
+            item.wait_recv()
+            total = total + rs[k + 1, :, span].astype(jnp.float32)
+        total = total.astype(jnp.bfloat16)
+        ag_out[:, span] = total
+        ag[ours, span] = total
+        out = []
+        for k in range(1, parts):
+            item = copy(
+                ag_out.at[:, span], ag.at[ours, span],
+                ag_s.at[which, k], ag_r.at[which, k], dom=mod(me + k, parts),
+            )
+            item.start()
+            out.append(item)
+        return out
+
+    at_node = contract_cols(ap[...], rt[...])
+    act_sum = at_node[:hid].astype(jnp.bfloat16)
+    recv_sum = at_node[hid:].astype(jnp.bfloat16)
+    sums[:, 2 * width:] = dot(act_sum, cf[...]).astype(jnp.bfloat16)
+    sums[:, width:2 * width] = dot(recv_sum, xf[...]).astype(jnp.bfloat16)
+    first = scatter(0)
+    near = contract_cols(ap[hid:], st_loc[...])
+    part_f[...] = dot(at_node[hid:].T.astype(jnp.bfloat16), win_ref[:, width:])
+
+    for item in b_copies:
+        item.wait_recv()
+    returned = back_in[...].astype(jnp.float32).T.astype(jnp.bfloat16)
+    whole = near + contract_cols(returned, lt[...])
+    sums[:, :width] = dot(whole.astype(jnp.bfloat16), xf[...]).astype(jnp.bfloat16)
+    second = scatter(1)
+    share = part_f[...] + dot(whole.T.astype(jnp.bfloat16), win_ref[:, :width])
+    part_f[...] = share
+    part_b[...] = share.astype(jnp.bfloat16)
+    p_copies = []
+    for k in range(1, tps):
+        peer = mod(mt + k, tps)
+        theirs = pl.ds(pl.multiple_of(peer * feat, feat), feat)
+        item = copy(part_b.at[:, theirs], part_in.at[k], p_s.at[k], p_r.at[k], tensor=peer)
+        item.start()
+        p_copies.append(item)
+
+    gathers = reduce(0, first)
+    node = c_ref[...].astype(jnp.float32) + part_f[:, mine]
+    for k, item in enumerate(p_copies):
+        item.wait_recv()
+        node = node + part_in[k + 1].astype(jnp.float32)
+    node_ref[...] = node.astype(jnp.bfloat16)
+    gathers += reduce(1, second)
+    for item in gathers:
+        item.wait_recv()
+    gin_ref[...] = ag[:, :2 * width].astype(jnp.float32) * scale
+    gout_ref[...] = ag[:, 2 * width:].astype(jnp.float32) * scale
+    for item in x_copies + c_copies + h_copies + b_copies + first + second + p_copies + gathers:
+        item.wait_send()
+
+
+def fused(node_state, cotangent, w_in, w_out, send_list, sender, receiver, edge_count):
+    parts = lax.axis_size("dom")
+    tps = lax.axis_size("tensor")
+    rows, feat = node_state.shape
+    hid = w_in.shape[0]
+    width = feat * tps
+    edges = sender.shape[0]
+    _, peers, slots = send_list.shape
+    halos = peers * slots
+    offsets = neighbour_offsets(parts)
+    chunk = hid // parts
+    scale = float(edges * parts) ** (-0.5)
+    bf16, f32 = jnp.bfloat16, jnp.float32
+    vm, dma = pltpu.VMEM, pltpu.SemaphoreType.DMA
+    spec = pl.BlockSpec(memory_space=pltpu.VMEM)
+    return pl.pallas_call(
+        functools.partial(layer_kernel, parts, tps, offsets, slots, scale),
+        out_shape=(
+            jax.ShapeDtypeStruct((rows, feat), bf16),
+            jax.ShapeDtypeStruct((hid, 2 * width), f32),
+            jax.ShapeDtypeStruct((hid, width), f32),
+        ),
+        in_specs=[spec] * 7 + [pl.BlockSpec(memory_space=pltpu.SMEM)],
+        out_specs=(spec, spec, spec),
+        scratch_shapes=[
+            vm((rows, width), bf16),
+            vm((rows, width), bf16),
+            vm((rows, edges), bf16),
+            vm((halos, edges), bf16),
+            vm((rows, edges), bf16),
+            vm((rows, halos), bf16),
+            vm((2 * hid, edges), bf16),
+            vm((hid, edges), f32),
+            vm((hid, edges), f32),
+            vm((halos, hid), f32),
+            vm((halos, hid), f32),
+            vm((halos, hid), bf16),
+            vm((halos, hid), bf16),
+            vm((hid, 3 * width), bf16),
+            vm((parts, chunk, 3 * width), bf16),
+            vm((chunk, 3 * width), bf16),
+            vm((hid, 3 * width), bf16),
+            vm((rows, width), f32),
+            vm((rows, width), bf16),
+            vm((tps, rows, feat), bf16),
+            dma((tps,)), dma((tps,)), dma((tps,)), dma((tps,)),
+            dma((peers,)), dma((peers,)), dma((peers,)), dma((peers,)),
+            dma((2, parts)), dma((2, parts)), dma((2, parts)), dma((2, parts)),
+            dma((tps,)), dma((tps,)),
+        ],
+        compiler_params=pltpu.CompilerParams(
+            collective_id=0, has_side_effects=True, vmem_limit_bytes=48 * 1024 * 1024
+        ),
+    )(
+        node_state, cotangent, w_in, w_out, send_list.reshape(1, halos),
+        sender.reshape(1, edges), receiver.reshape(1, edges), edge_count,
+    )
+
+
+def layer(node_state, cotangent, w_in, w_out, send_list, sender, receiver, edge_count):
+    parts = lax.axis_size("dom")
+    fits = (
+        node_state.shape[1] % 128 == 0
+        and node_state.shape[0] % 16 == 0
+        and send_list.shape[2] % 16 == 0
+        and w_in.shape[0] % (16 * parts) == 0
+        and sender.shape[0] % 128 == 0
+    )
+    plan = fused if fits else per_device
+    return plan(node_state, cotangent, w_in, w_out, send_list, sender, receiver, edge_count)
+
+
 def solution(mesh):
     return jax.shard_map(
-        per_device,
+        layer,
         mesh=mesh,
         in_specs=(
             P("dom", "tensor"),

time: 182 us -> 45.5 us (0.25)
  waiting for transfers between devices: 76.4 us -> 0 us
  Pallas kernels: 0 us -> 36.7 us
  starting transfers between devices: 26.3 us -> 0 us
  local copies, waits for them, and re-layouts: 29.8 us -> 6.44 us
  between operations: 16.5 us -> 1.32 us
  other arithmetic: 13.4 us -> 0.7 us
  blocking collectives: 12.4 us -> 0 us
  matrix products: 6.18 us -> 0 us
    psum x1 -> x0, waiting for transfers between devices: 71.1 us -> none  [per_device(): sum_in, sum_out = lax.psum((in_grad, out_grad), 'dom')]
    pallas_call x0 -> x1, Pallas kernels: none -> 36.7 us  [fused(): pl.pallas_call(functools.partial(layer_kernel, parts, tps, offsets, slots...]
    ppermute x14 -> x0, starting transfers between devices: 26.2 us -> none  [shifted(): return lax.ppermute(value, axis, pairs)]
    gather x10 -> x0, local copies, waits for them, and re-layouts: 25.5 us -> none  [the longest x7 9.91 us: per_device(): arrived.append(shifted(node_state[my_list[which]], 'dom', offset))]
    all_gather x2 -> x0, blocking collectives: 12.4 us -> none  [the longest x1 6.42 us: per_device(): lax.all_gather(table_part, 'tensor', axis=1, tiled=True)]
    dot_general x8 -> x0, matrix products: 6.18 us -> none  [the longest x3 2.16 us: contract_rows(): lax.dot_general(left, right, (((0,), (0,)), ((), ())), preferred_element_...]
    ppermute x14 -> x0, waiting for transfers between devices: 5.29 us -> none  [shifted(): return lax.ppermute(value, axis, pairs)]
    scatter-add x7 -> x0, other arithmetic: 5.15 us -> none  [per_device(): node_grad = node_grad.at[my_list[which]].add(returned)]
  transfers between devices with their start and end apart: 16 -> 0, of which waited for: 2 -> 0; matrix products, arithmetic and copies ran while one was open for 15% -> 0% of each run, Pallas kernels for 0% -> 0%
where the time goes in v1:
time: 45.5 us; the launch traced here: 45.2 us
  Pallas kernels  36.7 us (81%)
  local copies, waits for them, and re-layouts  6.44 us (14%)
  between operations  1.32 us (3%)
  other arithmetic  0.7 us (2%)
    pallas_call x1, Pallas kernels, fused(): pl.pallas_call(functools.partial(layer_kernel, parts, tps, offsets, slots...  36.7 us
    unnamed x15, local copies, waits for them, and re-layouts  6.35 us

profile of v1, /device:TPU:0, one launch (start us, length us, event | category | flops | bytes accessed | tf_op | source)
XLA Modules:
  0.0 45.2 jit_solution(18358059889191157976)
XLA Ops:
  0.6 0.0 copy-start.4
  1.3 0.7 %reduce = s32[7,16]{1,0:T(8,128)S(1)} reduce(s32[1,7,16]{2,0,1:T(1,128)} %param.12, s32[]{:T(128)} %constant.2), dimensions={0}, to_apply=%param.12.reduce_sub_computation | reduce | bytes 900 | tf_op args[4]
  2.0 0.1 reshape.15.list_ref
  2.1 0.0 copy-done.4
  2.1 0.0 copy-start.5
  2.1 0.7 %copy-done.5 = s32[1536]{0:T(1024)S(1)} copy-done((s32[1536]{0:T(1024)S(1)}, s32[1536]{0:T(1024)}, u32[]{:S(2)}) %copy-start.5) | copy-done | bytes 6168
  2.8 0.0 copy-start
  2.8 0.9 %copy-done = bf16[128,1024]{1,0:T(8,128)(2,1)S(1)} copy-done((bf16[128,1024]{1,0:T(8,128)(2,1)S(1)}, bf16[128,1024]{1,0:T(8,128)(2,1)}, u32[]{:S(2)}) %copy-start) | copy-done | bytes 262168
  3.7 0.0 copy-start.1
  3.7 0.9 %copy-done.1 = bf16[128,512]{1,0:T(8,128)(2,1)S(1)} copy-done((bf16[128,512]{1,0:T(8,128)(2,1)S(1)}, bf16[128,512]{1,0:T(8,128)(2,1)}, u32[]{:S(2)}) %copy-start.1) | copy-done | bytes 131096
  4.6 0.0 copy-start.2
  4.6 0.8 %copy-done.2 = bf16[256,128]{1,0:T(8,128)(2,1)S(1)} copy-done((bf16[256,128]{1,0:T(8,128)(2,1)S(1)}, bf16[256,128]{1,0:T(8,128)(2,1)}, u32[]{:S(2)}) %copy-start.2) | copy-done | bytes 65560
  5.5 0.0 copy-start.3
  5.5 0.8 %copy-done.3 = bf16[256,128]{1,0:T(8,128)(2,1)S(1)} copy-done((bf16[256,128]{1,0:T(8,128)(2,1)S(1)}, bf16[256,128]{1,0:T(8,128)(2,1)}, u32[]{:S(2)}) %copy-start.3) | copy-done | bytes 65560
  6.3 36.7 %shard_map.103 = (bf16[256,128]{1,0:T(8,128)(2,1)S(1)}, f32[128,1024]{1,0:T(8,128)S(1)}, f32[128,512]{1,0:T(8,128)S(1)}) custom-call(bf16[256,128]{1,0:T(8,128)(2,1)S(1)} %copy-done.2, bf16[256,128]{1,0:T(8,128)(2,1)S(1)} %copy-done.3, bf16[128,1024]{1,0:T(8,128)(2,1)S(1)} %copy-done, bf16[128,512]{1,0:T(8,128)(2,1)S(1)} %copy-done.1, ...), custom_call_target="tpu_custom_call" | custom-call | tf_op jit(solution)/shard_map/pallas_call | solution.py:302
  43.0 0.6 %copy.15 = bf16[256,128]{1,0:T(8,128)(2,1)} copy(bf16[256,128]{1,0:T(8,128)(2,1)S(1)} %get-tuple-element.6) | data formatting | bytes 131072
  43.7 0.8 %copy.16 = f32[128,1024]{1,0:T(8,128)} copy(f32[128,1024]{1,0:T(8,128)S(1)} %get-tuple-element.7) | data formatting | bytes 1048576
  44.5 0.7 %copy.17 = f32[128,512]{1,0:T(8,128)} copy(f32[128,512]{1,0:T(8,128)S(1)} %get-tuple-element.8) | data formatting | bytes 524288
  (2 shorter events, 0.0 us)
Async XLA Ops:
  0.6 1.5 %copy-start.4 = (s32[1536]{0:T(1024)S(1)}, s32[1536]{0:T(1024)}, u32[]{:S(2)}) copy-start(s32[1536]{0:T(1024)} %param.13) | copy-start | bytes 18436
  2.1 0.7 %copy-start.5 = (s32[1536]{0:T(1024)S(1)}, s32[1536]{0:T(1024)}, u32[]{:S(2)}) copy-start(s32[1536]{0:T(1024)} %param.14) | copy-start | bytes 18436
  2.8 0.9 %copy-start = (bf16[128,1024]{1,0:T(8,128)(2,1)S(1)}, bf16[128,1024]{1,0:T(8,128)(2,1)}, u32[]{:S(2)}) copy-start(bf16[128,1024]{1,0:T(8,128)(2,1)} %win_ref.1) | copy-start | bytes 786436
  3.7 0.9 %copy-start.1 = (bf16[128,512]{1,0:T(8,128)(2,1)S(1)}, bf16[128,512]{1,0:T(8,128)(2,1)}, u32[]{:S(2)}) copy-start(bf16[128,512]{1,0:T(8,128)(2,1)} %wout_ref.1) | copy-start | bytes 393220
  4.6 0.8 %copy-start.2 = (bf16[256,128]{1,0:T(8,128)(2,1)S(1)}, bf16[256,128]{1,0:T(8,128)(2,1)}, u32[]{:S(2)}) copy-start(bf16[256,128]{1,0:T(8,128)(2,1)} %x_ref.1) | copy-start | bytes 196612
  5.5 0.8 %copy-start.3 = (bf16[256,128]{1,0:T(8,128)(2,1)S(1)}, bf16[256,128]{1,0:T(8,128)(2,1)}, u32[]{:S(2)}) copy-start(bf16[256,128]{1,0:T(8,128)(2,1)} %c_ref.1) | copy-start | bytes 196612

commit v2 on v1

--- a/solution.py
+++ b/solution.py
@@ -96,10 +96,10 @@
 
 
 def layer_kernel(
-    parts, tps, offsets, slots, scale,
-    x_ref, c_ref, win_ref, wout_ref, list_ref, send_ref, recv_ref, count_ref,
-    node_ref, gin_ref, gout_ref,
-    xf, cf, st_loc, st_hal, rt, lt, ap, pre_buf, hid_buf,
+    parts, tps, offsets, slots,
+    x_ref, c_ref, win_any, wout_any, list_any, send_any, recv_any, count_ref,
+    node_ref, ag_ref,
+    win_ref, wout_ref, list_ref, send_ref, recv_ref, spot_ref, load_s, xf, cf, st_loc, st_hal, rt, lt, ap, pre_buf, hid_buf,
     halo_out, halo_in, back_out, back_in, sums, rs, ag_out, ag, part_f, part_b, part_in,
     gx_s, gx_r, gc_s, gc_r, h_s, h_r, b_s, b_r, rs_s, rs_r, ag_s, ag_r, p_s, p_r,
 ):
@@ -108,7 +108,7 @@
     rows, feat = x_ref.shape
     hid = win_ref.shape[0]
     width = feat * tps
-    edges = send_ref.shape[1]
+    edges = send_ref.shape[0]
     peers = len(offsets)
     halos = peers * slots
     chunk = hid // parts
@@ -129,9 +129,17 @@
         pl.semaphore_signal(barrier, inc=1, device_id={"tensor": mod(mt + k, tps)}, device_id_type=MESH)
     for k in range(1, parts):
         pl.semaphore_signal(barrier, inc=1, device_id={"dom": mod(me + k, parts)}, device_id_type=MESH)
+
+    mine = pl.ds(pl.multiple_of(mt * feat, feat), feat)
+    pairs = [
+        (list_any, list_ref), (send_any, send_ref), (recv_any, recv_ref),
+        (x_ref, xf.at[:, mine]), (win_any, win_ref), (c_ref, cf.at[:, mine]), (wout_any, wout_ref),
+    ]
+    loads = [pltpu.make_async_copy(a, b, load_s.at[i]) for i, (a, b) in enumerate(pairs)]
+    for item in loads:
+        item.start()
     pl.semaphore_wait(barrier, tps - 1 + parts - 1)
 
-    mine = pl.ds(pl.multiple_of(mt * feat, feat), feat)
     x_copies = [
         copy(x_ref, xf.at[:, mine], gx_s.at[k], gx_r.at[k], tensor=mod(mt + k, tps))
         for k in range(1, tps)
@@ -142,23 +150,28 @@
     ]
     for item in x_copies + c_copies:
         item.start()
-    xf[:, mine] = x_ref[...]
-    cf[:, mine] = c_ref[...]
 
     def hits(index, first, count):
         lanes = index.shape[1]
         spot = lax.broadcasted_iota(jnp.int32, (count, lanes), 0) + first
         return jnp.where(spot == index, 1.0, 0.0).astype(jnp.bfloat16)
 
-    lt[...] = hits(list_ref[...], 0, rows)
+    for item in loads[:3]:
+        item.wait()
+    for j in range(peers):
+        spot_ref[:, j * slots:(j + 1) * slots] = list_ref[j]
+    lt[...] = hits(spot_ref[...], 0, rows)
     count = count_ref[0]
     for cols in tiles:
         where = lax.broadcasted_iota(jnp.int32, (1, tile), 1) + cols.start
-        target = jnp.where(where < count, recv_ref[:, cols], -1)
+        target = jnp.where(where < count, recv_ref[cols].reshape(1, tile), -1)
         rt[:, cols] = hits(target, 0, rows)
-        st_loc[:, cols] = hits(send_ref[:, cols], 0, rows)
-        st_hal[:, cols] = hits(send_ref[:, cols], rows, halos)
-
+        sends = send_ref[cols].reshape(1, tile)
+        st_loc[:, cols] = hits(sends, 0, rows)
+        st_hal[:, cols] = hits(sends, rows, halos)
+
+    for item in loads[3:5]:
+        item.wait()
     for item in x_copies:
         item.wait_recv()
     own = split(contract_cols(win_ref[:, :width], xf[...]))
@@ -178,6 +191,8 @@
     for cols in tiles:
         both = dot(own, st_loc[:, cols]) + dot(at_recv, rt[:, cols])
         pre_buf[:, cols] = both[:hid] + both[hid:]
+    for item in loads[5:]:
+        item.wait()
     for item in c_copies:
         item.wait_recv()
     grad = split(contract_cols(wout_ref[...], cf[...]))
@@ -270,7 +285,7 @@
         p_copies.append(item)
 
     gathers = reduce(0, first)
-    node = c_ref[...].astype(jnp.float32) + part_f[:, mine]
+    node = cf[:, mine].astype(jnp.float32) + part_f[:, mine]
     for k, item in enumerate(p_copies):
         item.wait_recv()
         node = node + part_in[k + 1].astype(jnp.float32)
@@ -278,10 +293,24 @@
     gathers += reduce(1, second)
     for item in gathers:
         item.wait_recv()
-    gin_ref[...] = ag[:, :2 * width].astype(jnp.float32) * scale
-    gout_ref[...] = ag[:, 2 * width:].astype(jnp.float32) * scale
+    ag_ref[...] = ag[...]
     for item in x_copies + c_copies + h_copies + b_copies + first + second + p_copies + gathers:
         item.wait_send()
+
+
+def write_kernel(scale, node_ref, ag_ref, node_any, gin_any, gout_any, gin_ref, gout_ref, sems):
+    cut = gin_ref.shape[1]
+    node_copy = pltpu.make_async_copy(node_ref, node_any, sems.at[0])
+    node_copy.start()
+    gin_ref[...] = ag_ref[:, :cut].astype(jnp.float32) * scale
+    gin_copy = pltpu.make_async_copy(gin_ref, gin_any, sems.at[1])
+    gin_copy.start()
+    gout_ref[...] = ag_ref[:, cut:].astype(jnp.float32) * scale
+    gout_copy = pltpu.make_async_copy(gout_ref, gout_any, sems.at[2])
+    gout_copy.start()
+    node_copy.wait()
+    gin_copy.wait()
+    gout_copy.wait()
 
 
 def fused(node_state, cotangent, w_in, w_out, send_list, sender, receiver, edge_count):
@@ -299,16 +328,30 @@
     bf16, f32 = jnp.bfloat16, jnp.float32
     vm, dma = pltpu.VMEM, pltpu.SemaphoreType.DMA
     spec = pl.BlockSpec(memory_space=pltpu.VMEM)
-    return pl.pallas_call(
-        functools.partial(layer_kernel, parts, tps, offsets, slots, scale),
+    hbm = pl.BlockSpec(memory_space=pltpu.HBM)
+    operands = [
+        pltpu.with_memory_space_constraint(item, pltpu.HBM)
+        for item in (
+            node_state, cotangent, w_in, w_out, send_list.transpose(1, 0, 2),
+            sender, receiver,
+        )
+    ]
+    node, total = pl.pallas_call(
+        functools.partial(layer_kernel, parts, tps, offsets, slots),
         out_shape=(
             jax.ShapeDtypeStruct((rows, feat), bf16),
-            jax.ShapeDtypeStruct((hid, 2 * width), f32),
-            jax.ShapeDtypeStruct((hid, width), f32),
+            jax.ShapeDtypeStruct((hid, 3 * width), bf16),
         ),
-        in_specs=[spec] * 7 + [pl.BlockSpec(memory_space=pltpu.SMEM)],
-        out_specs=(spec, spec, spec),
+        in_specs=[hbm] * 7 + [pl.BlockSpec(memory_space=pltpu.SMEM)],
+        out_specs=(spec, spec),
         scratch_shapes=[
+            vm((hid, 2 * width), bf16),
+            vm((hid, width), bf16),
+            vm((peers, 1, slots), jnp.int32),
+            vm((edges,), jnp.int32),
+            vm((edges,), jnp.int32),
+            vm((1, halos), jnp.int32),
+            dma((7,)),
             vm((rows, width), bf16),
             vm((rows, width), bf16),
             vm((rows, edges), bf16),
@@ -338,9 +381,20 @@
             collective_id=0, has_side_effects=True, vmem_limit_bytes=48 * 1024 * 1024
         ),
     )(
-        node_state, cotangent, w_in, w_out, send_list.reshape(1, halos),
-        sender.reshape(1, edges), receiver.reshape(1, edges), edge_count,
-    )
+        *operands, edge_count
+    )
+    return pl.pallas_call(
+        functools.partial(write_kernel, scale),
+        out_shape=(
+            jax.ShapeDtypeStruct((rows, feat), bf16),
+            jax.ShapeDtypeStruct((hid, 2 * width), f32),
+            jax.ShapeDtypeStruct((hid, width), f32),
+        ),
+        in_specs=[spec, spec],
+        out_specs=(hbm, hbm, hbm),
+        scratch_shapes=[vm((hid, 2 * width), f32), vm((hid, width), f32), dma((3,))],
+        compiler_params=pltpu.CompilerParams(vmem_limit_bytes=4 * 1024 * 1024),
+    )(node, total)
 
 
 def layer(node_state, cotangent, w_in, w_out, send_list, sender, receiver, edge_count):

time: 45.5 us -> 39.4 us (0.87)
  local copies, waits for them, and re-layouts: 6.44 us -> 0 us
  Pallas kernels: 36.7 us -> 38 us
  other arithmetic: 0.7 us -> 0 us
    unnamed x15 -> x0, local copies, waits for them, and re-layouts: 6.35 us -> none
    pallas_call x0 -> x1, Pallas kernels: none -> 0.95 us  [fused(): pl.pallas_call(functools.partial(write_kernel, scale), out_shape=(jax.Sha...]
    unnamed x1 -> x0, other arithmetic: 0.7 us -> none
where the time goes in v2:
time: 39.4 us; the launch traced here: 39.2 us
  Pallas kernels  38 us (96%)
  between operations  1.29 us (3%)
    pallas_call x1, Pallas kernels, fused(): pl.pallas_call(functools.partial(layer_kernel, parts, tps, offsets, slots...  37 us
    pallas_call x1, Pallas kernels, fused(): pl.pallas_call(functools.partial(write_kernel, scale), out_shape=(jax.Sha...  0.95 us

profile of v2, /device:TPU:0, one launch (start us, length us, event | category | flops | bytes accessed | tf_op | source)
XLA Modules:
  0.0 39.2 jit_solution(2683609286920657578)
XLA Ops:
  1.3 37.0 %shard_map.103 = (bf16[256,128]{1,0:T(8,128)(2,1)S(1)}, bf16[128,1536]{1,0:T(8,128)(2,1)S(1)}) custom-call(bf16[256,128]{1,0:T(8,128)(2,1)} %x_ref.1, bf16[256,128]{1,0:T(8,128)(2,1)} %c_ref.1, bf16[128,1024]{1,0:T(8,128)(2,1)} %win_any.1, bf16[128,512]{1,0:T(8,128)(2,1)} %wout_any.1, s32[7,1,16]{2,1,0:T(1,128)} %bitcast.1, s32[1536]{0:T(1024)} %send_any.1, ...), custom_call_target="tpu_custom_call" | custom-call | tf_op jit(solution)/shard_map/pallas_call | solution.py:339
  38.3 0.9 %shard_map.104 = (bf16[256,128]{1,0:T(8,128)(2,1)}, f32[128,1024]{1,0:T(8,128)}, f32[128,512]{1,0:T(8,128)}) custom-call(bf16[256,128]{1,0:T(8,128)(2,1)S(1)} %get-tuple-element.5.node_ref, bf16[128,1536]{1,0:T(8,128)(2,1)S(1)} %get-tuple-element.6.ag_ref), custom_call_target="tpu_custom_call" | custom-call | tf_op jit(solution)/shard_map/pallas_call | solution.py:386

commit v3 on v2

--- a/solution.py
+++ b/solution.py
@@ -101,7 +101,7 @@
     node_ref, ag_ref,
     win_ref, wout_ref, list_ref, send_ref, recv_ref, spot_ref, load_s, xf, cf, st_loc, st_hal, rt, lt, ap, pre_buf, hid_buf,
     halo_out, halo_in, back_out, back_in, sums, rs, ag_out, ag, part_f, part_b, part_in,
-    gx_s, gx_r, gc_s, gc_r, h_s, h_r, b_s, b_r, rs_s, rs_r, ag_s, ag_r, p_s, p_r,
+    gx_s, gx_r, gc_s, gc_r, h_s, h_r, b_s, b_r, rs_s, rs_r, ag_s, ag_r, p_s, p_r, mid_out, mid_in, m_s, m_r,
 ):
     me = lax.axis_index("dom")
     mt = lax.axis_index("tensor")
@@ -111,7 +111,10 @@
     edges = send_ref.shape[0]
     peers = len(offsets)
     halos = peers * slots
-    chunk = hid // parts
+    squad = parts // 2
+    seat = lax.rem(me, squad)
+    base = me - seat
+    chunk = hid // squad
     tile = 512 if edges % 512 == 0 else edges
     tiles = [slice(i, i + tile) for i in range(0, edges, tile)]
 
@@ -226,33 +229,45 @@
 
     def scatter(which):
         out = []
-        for k in range(1, parts):
-            peer = mod(me + k, parts)
+        for k in range(1, squad):
+            peer = mod(seat + k, squad)
             band = pl.ds(pl.multiple_of(peer * chunk, chunk), chunk)
             item = copy(
                 sums.at[band, spans[which]], rs.at[k, :, spans[which]],
-                rs_s.at[which, k], rs_r.at[which, k], dom=peer,
+                rs_s.at[which, k], rs_r.at[which, k], dom=base + peer,
             )
             item.start()
             out.append(item)
         return out
 
-    ours = pl.ds(pl.multiple_of(me * chunk, chunk), chunk)
-
-    def reduce(which, arrivals):
+    ours = pl.ds(pl.multiple_of(seat * chunk, chunk), chunk)
+
+    def swap(which, arrivals):
         span = spans[which]
         total = sums[ours, span].astype(jnp.float32)
         for k, item in enumerate(arrivals):
             item.wait_recv()
             total = total + rs[k + 1, :, span].astype(jnp.float32)
+        mid_out[:, span] = total.astype(jnp.bfloat16)
+        item = copy(
+            mid_out.at[:, span], mid_in.at[:, span], m_s.at[which], m_r.at[which],
+            dom=mod(me + squad, parts),
+        )
+        item.start()
+        return item
+
+    def spread(which, arrival):
+        span = spans[which]
+        arrival.wait_recv()
+        total = mid_out[:, span].astype(jnp.float32) + mid_in[:, span].astype(jnp.float32)
         total = total.astype(jnp.bfloat16)
         ag_out[:, span] = total
         ag[ours, span] = total
         out = []
-        for k in range(1, parts):
+        for k in range(1, squad):
             item = copy(
                 ag_out.at[:, span], ag.at[ours, span],
-                ag_s.at[which, k], ag_r.at[which, k], dom=mod(me + k, parts),
+                ag_s.at[which, k], ag_r.at[which, k], dom=base + mod(seat + k, squad),
             )
             item.start()
             out.append(item)
@@ -284,17 +299,18 @@
         item.start()
         p_copies.append(item)
 
-    gathers = reduce(0, first)
+    swaps = [swap(0, first), swap(1, second)]
+    gathers = spread(0, swaps[0])
     node = cf[:, mine].astype(jnp.float32) + part_f[:, mine]
     for k, item in enumerate(p_copies):
         item.wait_recv()
         node = node + part_in[k + 1].astype(jnp.float32)
     node_ref[...] = node.astype(jnp.bfloat16)
-    gathers += reduce(1, second)
+    gathers += spread(1, swaps[1])
     for item in gathers:
         item.wait_recv()
     ag_ref[...] = ag[...]
-    for item in x_copies + c_copies + h_copies + b_copies + first + second + p_copies + gathers:
+    for item in x_copies + c_copies + h_copies + b_copies + first + second + p_copies + swaps + gathers:
         item.wait_send()
 
 
@@ -323,7 +339,8 @@
     _, peers, slots = send_list.shape
     halos = peers * slots
     offsets = neighbour_offsets(parts)
-    chunk = hid // parts
+    squad = parts // 2
+    chunk = hid // squad
     scale = float(edges * parts) ** (-0.5)
     bf16, f32 = jnp.bfloat16, jnp.float32
     vm, dma = pltpu.VMEM, pltpu.SemaphoreType.DMA
@@ -366,7 +383,7 @@
             vm((halos, hid), bf16),
             vm((halos, hid), bf16),
             vm((hid, 3 * width), bf16),
-            vm((parts, chunk, 3 * width), bf16),
+            vm((squad, chunk, 3 * width), bf16),
             vm((chunk, 3 * width), bf16),
             vm((hid, 3 * width), bf16),
             vm((rows, width), f32),
@@ -374,8 +391,9 @@
             vm((tps, rows, feat), bf16),
             dma((tps,)), dma((tps,)), dma((tps,)), dma((tps,)),
             dma((peers,)), dma((peers,)), dma((peers,)), dma((peers,)),
-            dma((2, parts)), dma((2, parts)), dma((2, parts)), dma((2, parts)),
+            dma((2, squad)), dma((2, squad)), dma((2, squad)), dma((2, squad)),
             dma((tps,)), dma((tps,)),
+            vm((chunk, 3 * width), bf16), vm((chunk, 3 * width), bf16), dma((2,)), dma((2,)),
         ],
         compiler_params=pltpu.CompilerParams(
             collective_id=0, has_side_effects=True, vmem_limit_bytes=48 * 1024 * 1024
@@ -403,6 +421,7 @@
         node_state.shape[1] % 128 == 0
         and node_state.shape[0] % 16 == 0
         and send_list.shape[2] % 16 == 0
+        and parts % 2 == 0
         and w_in.shape[0] % (16 * parts) == 0
         and sender.shape[0] % 128 == 0
     )

time: 39.4 us -> 36.1 us (0.916)
  Pallas kernels: 38 us -> 34.6 us
    pallas_call x1, Pallas kernels: 37 us -> 33.7 us  [fused(): pl.pallas_call(functools.partial(layer_kernel, parts, tps, offsets, slots...]
where the time goes in v3:
time: 36.1 us; the launch traced here: 35.9 us
  Pallas kernels  34.6 us (96%)
  between operations  1.29 us (4%)
    pallas_call x1, Pallas kernels, fused(): pl.pallas_call(functools.partial(layer_kernel, parts, tps, offsets, slots...  33.7 us
    pallas_call x1, Pallas kernels, fused(): pl.pallas_call(functools.partial(write_kernel, scale), out_shape=(jax.Sha...  0.95 us

profile of v3, /device:TPU:0, one launch (start us, length us, event | category | flops | bytes accessed | tf_op | source)
XLA Modules:
  0.0 35.9 jit_solution(9810490180015564928)
XLA Ops:
  1.3 33.7 %shard_map.103 = (bf16[256,128]{1,0:T(8,128)(2,1)S(1)}, bf16[128,1536]{1,0:T(8,128)(2,1)S(1)}) custom-call(bf16[256,128]{1,0:T(8,128)(2,1)} %x_ref.1, bf16[256,128]{1,0:T(8,128)(2,1)} %c_ref.1, bf16[128,1024]{1,0:T(8,128)(2,1)} %win_any.1, bf16[128,512]{1,0:T(8,128)(2,1)} %wout_any.1, s32[7,1,16]{2,1,0:T(1,128)} %bitcast.1, s32[1536]{0:T(1024)} %send_any.1, ...), custom_call_target="tpu_custom_call" | custom-call | tf_op jit(solution)/shard_map/pallas_call | solution.py:356
  35.0 0.9 %shard_map.104 = (bf16[256,128]{1,0:T(8,128)(2,1)}, f32[128,1024]{1,0:T(8,128)}, f32[128,512]{1,0:T(8,128)}) custom-call(bf16[256,128]{1,0:T(8,128)(2,1)S(1)} %get-tuple-element.5.node_ref, bf16[128,1536]{1,0:T(8,128)(2,1)S(1)} %get-tuple-element.6.ag_ref), custom_call_target="tpu_custom_call" | custom-call | tf_op jit(solution)/shard_map/pallas_call | solution.py:404

commit v4 on v3

--- a/solution.py
+++ b/solution.py
@@ -225,7 +225,7 @@
         item.start()
         b_copies.append(item)
 
-    spans = [slice(width, 3 * width), slice(0, width)]
+    spans = [slice(2 * width, 3 * width), slice(width, 2 * width), slice(0, width)]
 
     def scatter(which):
         out = []
@@ -277,8 +277,9 @@
     act_sum = at_node[:hid].astype(jnp.bfloat16)
     recv_sum = at_node[hid:].astype(jnp.bfloat16)
     sums[:, 2 * width:] = dot(act_sum, cf[...]).astype(jnp.bfloat16)
+    first = scatter(0)
     sums[:, width:2 * width] = dot(recv_sum, xf[...]).astype(jnp.bfloat16)
-    first = scatter(0)
+    second = scatter(1)
     near = contract_cols(ap[hid:], st_loc[...])
     part_f[...] = dot(at_node[hid:].T.astype(jnp.bfloat16), win_ref[:, width:])
 
@@ -287,7 +288,7 @@
     returned = back_in[...].astype(jnp.float32).T.astype(jnp.bfloat16)
     whole = near + contract_cols(returned, lt[...])
     sums[:, :width] = dot(whole.astype(jnp.bfloat16), xf[...]).astype(jnp.bfloat16)
-    second = scatter(1)
+    third = scatter(2)
     share = part_f[...] + dot(whole.T.astype(jnp.bfloat16), win_ref[:, :width])
     part_f[...] = share
     part_b[...] = share.astype(jnp.bfloat16)
@@ -301,16 +302,18 @@
 
     swaps = [swap(0, first), swap(1, second)]
     gathers = spread(0, swaps[0])
+    swaps.append(swap(2, third))
+    gathers += spread(1, swaps[1])
     node = cf[:, mine].astype(jnp.float32) + part_f[:, mine]
     for k, item in enumerate(p_copies):
         item.wait_recv()
         node = node + part_in[k + 1].astype(jnp.float32)
     node_ref[...] = node.astype(jnp.bfloat16)
-    gathers += spread(1, swaps[1])
+    gathers += spread(2, swaps[2])
     for item in gathers:
         item.wait_recv()
     ag_ref[...] = ag[...]
-    for item in x_copies + c_copies + h_copies + b_copies + first + second + p_copies + swaps + gathers:
+    for item in x_copies + c_copies + h_copies + b_copies + first + second + third + p_copies + swaps + gathers:
         item.wait_send()
 
 
@@ -391,9 +394,9 @@
             vm((tps, rows, feat), bf16),
             dma((tps,)), dma((tps,)), dma((tps,)), dma((tps,)),
             dma((peers,)), dma((peers,)), dma((peers,)), dma((peers,)),
-            dma((2, squad)), dma((2, squad)), dma((2, squad)), dma((2, squad)),
+            dma((3, squad)), dma((3, squad)), dma((3, squad)), dma((3, squad)),
             dma((tps,)), dma((tps,)),
-            vm((chunk, 3 * width), bf16), vm((chunk, 3 * width), bf16), dma((2,)), dma((2,)),
+            vm((chunk, 3 * width), bf16), vm((chunk, 3 * width), bf16), dma((3,)), dma((3,)),
         ],
         compiler_params=pltpu.CompilerParams(
             collective_id=0, has_side_effects=True, vmem_limit_bytes=48 * 1024 * 1024

time: 36.1 us -> 36 us (level)
  no operation moved by 1% of the time
where the time goes in v4:
time: 36 us; the launch traced here: 35.9 us
  Pallas kernels  34.6 us (96%)
  between operations  1.29 us (4%)
    pallas_call x1, Pallas kernels, fused(): pl.pallas_call(functools.partial(layer_kernel, parts, tps, offsets, slots...  33.6 us
    pallas_call x1, Pallas kernels, fused(): pl.pallas_call(functools.partial(write_kernel, scale), out_shape=(jax.Sha...  0.95 us

profile of v4, /device:TPU:0, one launch (start us, length us, event | category | flops | bytes accessed | tf_op | source)
XLA Modules:
  0.0 35.9 jit_solution(394187318889064535)
XLA Ops:
  1.3 33.6 %shard_map.103 = (bf16[256,128]{1,0:T(8,128)(2,1)S(1)}, bf16[128,1536]{1,0:T(8,128)(2,1)S(1)}) custom-call(bf16[256,128]{1,0:T(8,128)(2,1)} %x_ref.1, bf16[256,128]{1,0:T(8,128)(2,1)} %c_ref.1, bf16[128,1024]{1,0:T(8,128)(2,1)} %win_any.1, bf16[128,512]{1,0:T(8,128)(2,1)} %wout_any.1, s32[7,1,16]{2,1,0:T(1,128)} %bitcast.1, s32[1536]{0:T(1024)} %send_any.1, ...), custom_call_target="tpu_custom_call" | custom-call | tf_op jit(solution)/shard_map/pallas_call | solution.py:359
  34.9 0.9 %shard_map.104 = (bf16[256,128]{1,0:T(8,128)(2,1)}, f32[128,1024]{1,0:T(8,128)}, f32[128,512]{1,0:T(8,128)}) custom-call(bf16[256,128]{1,0:T(8,128)(2,1)S(1)} %get-tuple-element.5.node_ref, bf16[128,1536]{1,0:T(8,128)(2,1)S(1)} %get-tuple-element.6.ag_ref), custom_call_target="tpu_custom_call" | custom-call | tf_op jit(solution)/shard_map/pallas_call | solution.py:407

commit v5 on v4

--- a/solution.py
+++ b/solution.py
@@ -209,7 +209,7 @@
     for cols in tiles:
         both = dot(far, st_hal[:, cols])
         pre = pre_buf[:, cols] + both[:hid] + both[hid:]
-        sig = jax.nn.sigmoid(pre)
+        sig = 0.5 * jnp.tanh(0.5 * pre) + 0.5
         slope = sig * (1.0 + pre * (1.0 - sig))
         ap[:hid, cols] = (pre * sig).astype(jnp.bfloat16)
         ap[hid:, cols] = (hid_buf[:, cols] * slope).astype(jnp.bfloat16)

time: 36 us -> 36.1 us (level)
  no operation moved by 1% of the time
where the time goes in v5:
time: 36.1 us; the launch traced here: 35.9 us
  Pallas kernels  34.6 us (96%)
  between operations  1.29 us (4%)
    pallas_call x1, Pallas kernels, fused(): pl.pallas_call(functools.partial(layer_kernel, parts, tps, offsets, slots...  33.7 us
    pallas_call x1, Pallas kernels, fused(): pl.pallas_call(functools.partial(write_kernel, scale), out_shape=(jax.Sha...  0.95 us

profile of v5, /device:TPU:0, one launch (start us, length us, event | category | flops | bytes accessed | tf_op | source)
XLA Modules:
  0.0 35.9 jit_solution(3183078694592523627)
XLA Ops:
  1.3 33.7 %shard_map.103 = (bf16[256,128]{1,0:T(8,128)(2,1)S(1)}, bf16[128,1536]{1,0:T(8,128)(2,1)S(1)}) custom-call(bf16[256,128]{1,0:T(8,128)(2,1)} %x_ref.1, bf16[256,128]{1,0:T(8,128)(2,1)} %c_ref.1, bf16[128,1024]{1,0:T(8,128)(2,1)} %win_any.1, bf16[128,512]{1,0:T(8,128)(2,1)} %wout_any.1, s32[7,1,16]{2,1,0:T(1,128)} %bitcast.1, s32[1536]{0:T(1024)} %send_any.1, ...), custom_call_target="tpu_custom_call" | custom-call | tf_op jit(solution)/shard_map/pallas_call | solution.py:359
  35.0 0.9 %shard_map.104 = (bf16[256,128]{1,0:T(8,128)(2,1)}, f32[128,1024]{1,0:T(8,128)}, f32[128,512]{1,0:T(8,128)}) custom-call(bf16[256,128]{1,0:T(8,128)(2,1)S(1)} %get-tuple-element.5.node_ref, bf16[128,1536]{1,0:T(8,128)(2,1)S(1)} %get-tuple-element.6.ag_ref), custom_call_target="tpu_custom_call" | custom-call | tf_op jit(solution)/shard_map/pallas_call | solution.py:407
